TPU v7x, 256 devices: a whole 4x4x8 slice. The times are simulated.
256 devices in a mesh: rows: 32 (over y, x, core), cols: 8 (over z).
Axes of the slice: x: 4, y: 4, z: 8, core: 2. Of those that a mesh axis runs over, the one named last changes fastest.
Arguments:
- eigvecs: float32 [65536, 4096], P('rows', 'cols'), may hold values from -6 to 6
- reflectors: float32 [4, 65536, 256], P(None, 'rows', 'cols'), may hold values from -0.0234375 to 0.0234375
- t_factors: float32 [4, 256, 256], replicated, may hold values from -1 to 3, as said below
Outputs:
- transformed: float32 [65536, 4096], P('rows', 'cols')
Inputs may be any that keep to these rules, and one draw needn't show every extreme that they name: Each t_factors[p] is upper triangular with a diagonal between 1 and 3.
All inputs are finite; a program needn't handle non-finite values.
Results may differ from a plain program's by a relative error of at most 0.00011.
Values sent between devices are 32-bit elements; how exact they have to be, the bound alone decides.
A program may use at most 64 MiB of HBM per device.

v0:
```python
import jax
import jax.numpy as jnp
from jax import lax
from jax.sharding import PartitionSpec as P


def inner_rows(panel, field):
    return lax.dot_general(
        panel,
        field,
        (((0,), (0,)), ((), ())),
        precision=lax.Precision.HIGHEST,
        preferred_element_type=jnp.float32,
    )


def matmul(left, right):
    return jnp.dot(left, right, precision=lax.Precision.HIGHEST, preferred_element_type=jnp.float32)


def reduce_columns(first_inner, combine):
    sums = lax.psum(first_inner, "rows")
    return combine(sums, None, None)


def body(eigvecs, reflectors, t_factors):
    panels_full = lax.all_gather(reflectors, "cols", axis=2, tiled=True)
    total = panels_full.shape[0]
    field = eigvecs
    for index in range(total):
        panel = panels_full[index]
        factor = t_factors[index]

        def solve_single(sums, unused_second, unused_correlation, factor=factor):
            return matmul(factor, sums)

        coeffs = reduce_columns(inner_rows(panel, field), solve_single)
        field = field - matmul(panel, coeffs)
    return field


def solution(mesh):
    in_specs = (P("rows", "cols"), P(None, "rows", "cols"), P())
    out_specs = P("rows", "cols")
    return jax.shard_map(body, mesh=mesh, in_specs=in_specs, out_specs=out_specs, check_vma=False)
```

profile of v0, /device:TPU:1, one launch (start us, length us, event | category | flops | bytes accessed | tf_op | source)
XLA Modules:
  0.0 635.3 jit_solution(1386079602272724529)
XLA Ops:
  6.5 0.7 all-gather.2.cloned.1.call-update
  7.3 99.8 %all-gather.2.cloned.1.call-done = f32[4,2048,256]{1,2,0:T(8,128)} async-done(((f32[4,2048,32]{1,2,0:T(8,128)}), f32[4,2048,256]{1,2,0:T(8,128)}) %all-gather.2.cloned.1.call-update) | async-done | bytes 8388624 | tf_op jit(solution)/shard_map/all_gather | solution.py:27
  107.1 7.3 %fusion = f32[256,512]{1,0:T(8,128)} fusion(f32[2048,512]{1,0:T(8,128)} %param.3, f32[4,2048,256]{1,2,0:T(8,128)} %all-gather.2.cloned.1.call-done), kind=kOutput, calls=%fused_computation.8 | convolution fusion | flops 3221225472 | bytes 6815744 | tf_op jit(solution)/shard_map/dot_general | solution.py:8
  114.5 5.4 copy.4
  119.9 106.9 %all-reduce.5.cloned.1.call-done = f32[256,512]{1,0:T(8,128)} async-done(((f32[256,512]{1,0:T(8,128)}), f32[256,512]{1,0:T(8,128)}) %all-reduce.5.cloned.1.call-update) | async-done | bytes 524304 | tf_op jit(solution)/shard_map/psum | solution.py:22
  226.8 2.0 fusion.13
  228.9 6.2 bitcast_subtract_fusion.3
  235.1 2.0 copy-done
  237.1 5.9 fusion.6
  243.2 113.0 %all-reduce.7.cloned.1.call-done = f32[256,512]{0,1:T(8,128)} async-done(((f32[256,512]{0,1:T(8,128)}), f32[256,512]{0,1:T(8,128)}) %all-reduce.7.cloned.1.call-update) | async-done | bytes 524304 | tf_op jit(solution)/shard_map/psum | solution.py:22
  356.3 1.7 fusion.11
  357.9 6.2 bitcast_subtract_fusion.2
  364.1 2.0 copy-done.1
  366.1 5.9 fusion.5
  372.1 0.3 all-reduce.11.cloned.1.call-start
  372.3 113.0 %all-reduce.9.cloned.1.call-done = f32[256,512]{0,1:T(8,128)} async-done(((f32[256,512]{0,1:T(8,128)}), f32[256,512]{0,1:T(8,128)}) %all-reduce.9.cloned.1.call-update) | async-done | bytes 524304 | tf_op jit(solution)/shard_map/psum | solution.py:22
  485.3 1.7 fusion.9
  487.0 6.2 bitcast_subtract_fusion.1
  493.2 2.0 copy-done.2
  495.2 5.9 fusion.4
  501.1 113.3 %all-reduce.11.cloned.1.call-done = f32[256,512]{0,1:T(8,128)} async-done(((f32[256,512]{0,1:T(8,128)}), f32[256,512]{0,1:T(8,128)}) %all-reduce.11.cloned.1.call-update) | async-done | bytes 524304 | tf_op jit(solution)/shard_map/psum | solution.py:22
  614.4 1.7 fusion.7
  616.1 7.4 %bitcast_subtract_fusion = f32[2048,512]{0,1:T(8,128)} fusion(f32[2048,512]{0,1:T(8,128)} %copy-done.2, f32[512,256]{1,0:T(8,128)S(1)} %fusion.7, f32[4,2048,256]{1,2,0:T(8,128)} %all-gather.2.cloned.1.call-done), kind=kOutput, calls=%fused_computation | convolution fusion | flops 3222274048 | bytes 11010048 | tf_op jit(solution)/shard_map/dot_general | solution.py:18
  623.4 5.3 copy.5
  (13 shorter events, 0.4 us)
Async XLA Ops:
  6.5 100.6 %all-gather.2.cloned.1.call-start = ((), (), s32[]{:S(2)}) async-start(), calls=%async_computation | async-start | bytes 9437184 | tf_op jit(solution)/shard_map/all_gather | solution.py:27
  7.3 219.6 %all-reduce.5.cloned.1.call-start = ((), (), s32[]{:S(2)}) async-start(), calls=%async_computation.1 | async-start | bytes 1048576 | tf_op jit(solution)/shard_map/psum | solution.py:22
  114.5 112.4 %copy-start.3 = (f32[4,256,256]{2,1,0:T(8,128)S(1)}, f32[4,256,256]{2,1,0:T(8,128)}, u32[]{:S(2)}) copy-start(f32[4,256,256]{2,1,0:T(8,128)} %param.5) | copy-start | bytes 3145732
  114.5 241.8 %all-reduce.7.cloned.1.call-start = ((), (), s32[]{:S(2)}) async-start(), calls=%async_computation.2 | async-start | bytes 1048576 | tf_op jit(solution)/shard_map/psum | solution.py:22
  235.0 2.0 copy-start
  243.0 242.3 %all-reduce.9.cloned.1.call-start = ((), (), s32[]{:S(2)}) async-start(), calls=%async_computation.3 | async-start | bytes 1048576 | tf_op jit(solution)/shard_map/psum | solution.py:22
  364.1 2.0 copy-start.1
  372.1 242.3 %all-reduce.11.cloned.1.call-start = ((), (), s32[]{:S(2)}) async-start(), calls=%async_computation.4 | async-start | bytes 1048576 | tf_op jit(solution)/shard_map/psum | solution.py:22
  493.2 2.0 copy-start.2
Sparse Core Ops, SparseCore 0:
  9.1 97.8 all-gather.1
  114.6 112.1 all-reduce.4
  243.1 113.1 all-reduce.6
  372.2 113.0 all-reduce.8
  501.2 113.1 all-reduce.10
where the time goes:
time: 636 us; the launch traced here: 635 us
  waiting for transfers between devices  547 us (86%)
  matrix products  57.9 us (9%)
  local copies, waits for them, and re-layouts  16.8 us (3%)
  between operations  13.2 us (2%)
    psum x4, waiting for transfers between devices, reduce_columns(): sums = lax.psum(first_inner, 'rows')  446 us
    all_gather x1, waiting for transfers between devices, body(): panels_full = lax.all_gather(reflectors, 'cols', axis=2, tiled=True)  99.8 us
    dot_general x8, matrix products, matmul(): jnp.dot(left, right, precision=lax.Precision.HIGHEST, preferred_element_t...  32.9 us
    dot_general x4, matrix products, inner_rows(): lax.dot_general(panel, field, (((0,), (0,)), ((), ())), precision=lax.Pre...  25.1 us
  transfers between devices with their start and end apart: 5, of which 5 were waited for; matrix products, arithmetic and copies ran while one was open for 1% of the time, Pallas kernels for 0%

commit v1 on v0

v1 whole, which is shorter than its diff:
```python
import functools

import jax
import jax.numpy as jnp
from jax import lax
from jax.experimental import pallas as pl
from jax.experimental.pallas import tpu as pltpu
from jax.sharding import PartitionSpec as P

MESH = pl.DeviceIdType.MESH
F32, BF16 = jnp.float32, jnp.bfloat16
PIECE = 8
TILE = 256


def halves(value):
    high = value.astype(BF16)
    return high, (value - high.astype(F32)).astype(BF16)


def product(left, right):
    (left_high, left_low), (right_high, right_low) = left, right
    dot = functools.partial(jnp.dot, preferred_element_type=F32)
    return dot(left_high, right_high) + (dot(left_high, right_low) + dot(left_low, right_high))


def kernel(
    field_in, refl_in, factor_in, out_ref,
    panel, field, high, low, plain_high, plain_low, factors, coef_high, coef_low,
    part, pair, half, spread, sums,
    z_send, z_recv, rs_send, rs_recv, ag_send, ag_recv, core_send, core_recv, own_sem, in_sem, out_sem,
):
    row, z = lax.axis_index("rows"), lax.axis_index("cols")
    core, chip = row % 2, row // 2
    x, y = chip % 4, chip // 4
    z_next = ((row, (z + 1) % 8), (row, (z + 7) % 8))
    twin = (chip * 2 + 1 - core, z)

    def chip_at(k):
        return ((y + k // 4) % 4) * 4 + (x + k % 4) % 4

    def chip_device(k):
        return (chip_at(k) * 2 + core, z)

    panels, blocks = panel.shape[0], field.shape[0] // TILE

    load_field = pltpu.make_async_copy(field_in, field, in_sem.at[0])
    load_factors = pltpu.make_async_copy(factor_in, factors, in_sem.at[1])
    load_field.start()
    load_factors.start()

    def own(p, c):
        return pltpu.make_async_copy(refl_in.at[p, pl.ds(PIECE * c, PIECE)], panel.at[p, z * 4 + c], own_sem.at[p, c])

    for p in range(panels):
        for c in range(4):
            own(p, c).start()

    barrier = pltpu.get_barrier_semaphore()
    for device in (*z_next, twin):
        pl.semaphore_signal(barrier, inc=1, device_id=device, device_id_type=MESH)

    def greet(k, carry):
        pl.semaphore_signal(barrier, inc=1, device_id=chip_device(k), device_id_type=MESH)
        return carry

    lax.fori_loop(1, 16, greet, 0)
    load_field.wait()

    def split(i, carry):
        rows = pl.ds(pl.multiple_of(i * TILE, TILE), TILE)
        high[rows, :], low[rows, :] = halves(field[rows, :])
        return carry

    lax.fori_loop(0, blocks, split, 0)
    pl.semaphore_wait(barrier, 18)

    def hop(p, way, s, c):
        c = c if way == 0 else 3 - c
        owner = (z + 8 - s) % 8 if way == 0 else (z + s) % 8
        source = refl_in.at[p, pl.ds(PIECE * c, PIECE)] if s == 0 else panel.at[p, owner * 4 + c]
        return pltpu.make_async_remote_copy(
            src_ref=source, dst_ref=panel.at[p, owner * 4 + c],
            send_sem=z_send.at[p, way, s, c], recv_sem=z_recv.at[p, way, s, c],
            device_id=z_next[way], device_id_type=MESH,
        )

    def landed(p, way, s, c):
        c = c if way == 0 else 3 - c
        owner = (z + 7 - s) % 8 if way == 0 else (z + 1 + s) % 8
        place = panel.at[p, owner * 4 + c]
        pltpu.make_async_remote_copy(
            src_ref=place, dst_ref=place,
            send_sem=z_send.at[p, way, s, c], recv_sem=z_recv.at[p, way, s, c],
            device_id=z_next[way], device_id_type=MESH,
        ).wait_recv()

    def slots(p, first, last):
        for i in range(first, last):
            s, c = i // 4, i % 4
            for way in (0, 1):
                if s:
                    landed(p, way, s - 1, c)
                hop(p, way, s, c).start()

    def finals(p):
        for way in (0, 1):
            for s, c in ((2, 2), (2, 3), (3, 0), (3, 1)):
                landed(p, way, s, c)
        for c in range(4):
            own(p, c).wait()

    def inner(p, first, last):
        def step(i, carry):
            rows = pl.ds(pl.multiple_of(i * TILE, TILE), TILE)
            left = halves(panel[p, :, :, rows].reshape(256, TILE))
            term = product(left, (high[rows, :], low[rows, :])).reshape(part.shape[1:])
            if first == 0:
                part[p] = jnp.where(i == 0, term, part[p] + term)
            else:
                part[p] += term
            return carry

        lax.fori_loop(first, last, step, 0)

    def turn(p, first, last):
        def step(i, carry):
            rows = pl.ds(pl.multiple_of(i * TILE, TILE), TILE)
            plain_high[rows, :], plain_low[rows, :] = halves(panel[p, :, :, rows].reshape(256, TILE).T)
            return carry

        lax.fori_loop(first, last, step, 0)

    def to_twin(p, which, source, target):
        return pltpu.make_async_remote_copy(
            src_ref=source, dst_ref=target, send_sem=core_send.at[p, which], recv_sem=core_recv.at[p, which],
            device_id=twin, device_id_type=MESH,
        )

    def exchange(p):
        return to_twin(p, 0, part.at[p, pl.ds((1 - core) * 16, 16)], pair.at[p])

    def scatter(p, k):
        return pltpu.make_async_remote_copy(
            src_ref=half.at[p, chip_at(k)], dst_ref=spread.at[p, k], send_sem=rs_send.at[p, k], recv_sem=rs_recv.at[p, k],
            device_id=chip_device(k), device_id_type=MESH,
        )

    def share(p, k):
        mine = sums.at[p, core * 16 + chip]
        return pltpu.make_async_remote_copy(
            src_ref=mine, dst_ref=mine, send_sem=ag_send.at[p, k], recv_sem=ag_recv.at[p, k],
            device_id=chip_device(k), device_id_type=MESH,
        )

    def shared(p, k):
        theirs = sums.at[p, core * 16 + ((y + 4 - k // 4) % 4) * 4 + (x + 4 - k % 4) % 4]
        return pltpu.make_async_remote_copy(
            src_ref=theirs, dst_ref=theirs, send_sem=ag_send.at[p, k], recv_sem=ag_recv.at[p, k],
            device_id=chip_device(k), device_id_type=MESH,
        )

    def each(action):
        def step(k, carry):
            action(k)
            return carry

        lax.fori_loop(1, 16, step, 0)

    def pair_sum(p):
        exchange(p).wait_recv()
        half[p] = part[p, pl.ds(core * 16, 16)] + pair[p]

    def chip_sum(p):
        each(lambda k: scatter(p, k).wait_recv())
        total = half[p, chip]
        for k in range(1, 16):
            total = total + spread[p, k]
        sums[p, core * 16 + chip] = total

    def join(p):
        each(lambda k: shared(p, k).wait_recv())
        mine = sums.at[p, pl.ds(core * 16, 16)]
        to_twin(p, 1, mine, mine).start()

    def coefficients(p):
        theirs = sums.at[p, pl.ds((1 - core) * 16, 16)]
        to_twin(p, 1, theirs, theirs).wait_recv()
        coef = jnp.dot(factors[p], sums[p].reshape(256, -1), precision=lax.Precision.HIGHEST, preferred_element_type=F32)
        coef_high[...], coef_low[...] = halves(coef)

    def update(p, last):
        def step(i, carry):
            rows = pl.ds(pl.multiple_of(i * TILE, TILE), TILE)
            fresh = field[rows, :] - product((plain_high[rows, :], plain_low[rows, :]), (coef_high[...], coef_low[...]))
            field[rows, :] = fresh
            if last:
                pltpu.make_async_copy(field.at[rows], out_ref.at[rows], out_sem.at[i]).start()
            else:
                high[rows, :], low[rows, :] = halves(fresh)
            return carry

        lax.fori_loop(0, blocks, step, 0)

    def chain(p, slot, last):
        finals(p)
        inner(p, 0, 3)
        slot(4, 5)
        inner(p, 3, 6)
        slot(5, 6)
        inner(p, 6, 8)
        exchange(p).start()
        slot(6, 7)
        pair_sum(p)
        each(lambda k: scatter(p, k).start())
        for i in range(4):
            turn(p, 2 * i, 2 * i + 2)
            slot(7 + i, 8 + i)
        chip_sum(p)
        each(lambda k: share(p, k).start())
        slot(11, 14)

    def finish(p, last):
        join(p)
        coefficients(p)
        update(p, last)

    load_factors.wait()
    slots(0, 0, 14)

    def turn_of_panel(p, carry):
        slots(p, 0, 4)

        @pl.when(p > 1)
        def _():
            finish(p - 2, False)

        chain(p - 1, functools.partial(slots, p), False)
        return carry

    lax.fori_loop(1, panels, turn_of_panel, 0)
    finish(panels - 2, False)
    chain(panels - 1, lambda first, last: None, True)
    finish(panels - 1, True)

    def drain(p, carry):
        for way in (0, 1):
            for i in range(14):
                hop(p, way, i // 4, i % 4).wait_send()
        exchange(p).wait_send()
        mine = sums.at[p, pl.ds(core * 16, 16)]
        to_twin(p, 1, mine, mine).wait_send()
        each(lambda k: scatter(p, k).wait_send())
        each(lambda k: share(p, k).wait_send())
        return carry

    lax.fori_loop(0, panels, drain, 0)

    def written(i, carry):
        rows = pl.ds(pl.multiple_of(i * TILE, TILE), TILE)
        pltpu.make_async_copy(field.at[rows], out_ref.at[rows], out_sem.at[i]).wait()
        return carry

    lax.fori_loop(0, blocks, written, 0)


def body(eigvecs, reflectors, t_factors):
    rows, columns = eigvecs.shape
    panels, block = t_factors.shape[:2]
    dma, vmem = pltpu.SemaphoreType.DMA, pltpu.VMEM
    return pl.pallas_call(
        kernel,
        out_shape=jax.ShapeDtypeStruct((rows, columns), F32),
        in_specs=[pl.BlockSpec(memory_space=pl.ANY)] * 3,
        out_specs=pl.BlockSpec(memory_space=pl.ANY),
        scratch_shapes=[
            vmem((panels, block // PIECE, PIECE, rows), F32),
            vmem((rows, columns), F32),
            vmem((rows, columns), BF16),
            vmem((rows, columns), BF16),
            vmem((rows, block), BF16),
            vmem((rows, block), BF16),
            vmem((panels, block, block), F32),
            vmem((block, columns), BF16),
            vmem((block, columns), BF16),
            vmem((panels, 32, 8, columns), F32),
            vmem((panels, 16, 8, columns), F32),
            vmem((panels, 16, 8, columns), F32),
            vmem((panels, 16, 8, columns), F32),
            vmem((panels, 32, 8, columns), F32),
            dma((panels, 2, 4, 4)),
            dma((panels, 2, 4, 4)),
            dma((panels, 16)),
            dma((panels, 16)),
            dma((panels, 16)),
            dma((panels, 16)),
            dma((panels, 2)),
            dma((panels, 2)),
            dma((panels, 4)),
            dma((2,)),
            dma((rows // TILE,)),
        ],
        compiler_params=pltpu.CompilerParams(collective_id=0, has_side_effects=True, vmem_limit_bytes=56 * 2**20),
        cost_estimate=pl.CostEstimate(flops=13 * 10**9, bytes_accessed=10 * 2**20, transcendentals=0),
    )(eigvecs, jnp.swapaxes(reflectors, 1, 2), t_factors)


def solution(mesh):
    in_specs = (P("rows", "cols"), P(None, "rows", "cols"), P())
    return jax.shard_map(body, mesh=mesh, in_specs=in_specs, out_specs=P("rows", "cols"), check_vma=False)
```

time: 636 us -> 130 us (0.20)
  waiting for transfers between devices: 547 us -> 0 us
  Pallas kernels: 0 us -> 125 us
  matrix products: 57.9 us -> 0 us
  between operations: 13.2 us -> 0.01 us
  local copies, waits for them, and re-layouts: 16.8 us -> 4.64 us
    psum x4 -> x0, waiting for transfers between devices: 446 us -> none  [reduce_columns(): sums = lax.psum(first_inner, 'rows')]
    pallas_call x0 -> x1, Pallas kernels: none -> 125 us  [body(): pl.pallas_call(kernel, out_shape=jax.ShapeDtypeStruct((rows, columns), F3...]
    all_gather x1 -> x0, waiting for transfers between devices: 99.8 us -> none  [body(): panels_full = lax.all_gather(reflectors, 'cols', axis=2, tiled=True)]
    dot_general x12 -> x0, matrix products: 57.9 us -> none  [the longest x8 32.9 us: matmul(): jnp.dot(left, right, precision=lax.Precision.HIGHEST, preferred_element_t...]
    unnamed x9 -> x1, local copies, waits for them, and re-layouts: 11.5 us -> 4.64 us
  transfers between devices with their start and end apart: 5 -> 0, of which waited for: 5 -> 0; matrix products, arithmetic and copies ran while one was open for 1% -> 0% of each run, Pallas kernels for 0% -> 0%
where the time goes in v1:
time: 130 us
  Pallas kernels  125 us (96%)
  local copies, waits for them, and re-layouts  4.64 us (4%)
    pallas_call x1, Pallas kernels, body(): pl.pallas_call(kernel, out_shape=jax.ShapeDtypeStruct((rows, columns), F3...  125 us
    unnamed x1, local copies, waits for them, and re-layouts  4.64 us

profile of v1, /device:TPU:1, one launch (start us, length us, event | category | flops | bytes accessed | tf_op | source)
XLA Modules:
  0.0 129.6 jit_solution(1540085308775144486)
XLA Ops:
  0.0 124.9 %shard_map.37 = f32[2048,512]{1,0:T(8,128)} custom-call(f32[2048,512]{1,0:T(8,128)} %field_in.1, f32[4,32,2048]{2,1,0:T(8,128)} %bitcast.1, f32[4,256,256]{2,1,0:T(8,128)} %factor_in.1), custom_call_target="tpu_custom_call" | custom-call | flops 12999999488 | bytes 10485760 | tf_op jit(solution)/shard_map/pallas_call | solution.py:271
  124.9 4.6 %copy.5 = f32[2048,512]{1,0:T(8,128)} copy(f32[2048,512]{1,0:T(8,128)} %shard_map.37) | data formatting | bytes 8388608

commit v2 on v1

--- a/solution.py
+++ b/solution.py
@@ -25,10 +25,11 @@
 
 
 def kernel(
-    field_in, refl_in, factor_in, out_ref,
-    panel, field, high, low, plain_high, plain_low, factors, coef_high, coef_low,
+    field_in, refl_in, factor_in,
+    field, plain_high, plain_low, coef_high, coef_low,
+    panel, high, low, factors,
     part, pair, half, spread, sums,
-    z_send, z_recv, rs_send, rs_recv, ag_send, ag_recv, core_send, core_recv, own_sem, in_sem, out_sem,
+    z_send, z_recv, rs_send, rs_recv, ag_send, ag_recv, core_send, core_recv, own_sem, in_sem,
 ):
     row, z = lax.axis_index("rows"), lax.axis_index("cols")
     core, chip = row % 2, row // 2
@@ -65,14 +66,11 @@
         return carry
 
     lax.fori_loop(1, 16, greet, 0)
-    load_field.wait()
-
     def split(i, carry):
         rows = pl.ds(pl.multiple_of(i * TILE, TILE), TILE)
         high[rows, :], low[rows, :] = halves(field[rows, :])
         return carry
 
-    lax.fori_loop(0, blocks, split, 0)
     pl.semaphore_wait(barrier, 18)
 
     def hop(p, way, s, c):
@@ -95,13 +93,15 @@
             device_id=z_next[way], device_id_type=MESH,
         ).wait_recv()
 
-    def slots(p, first, last):
+    def slots(p, first, last, settle=True):
         for i in range(first, last):
             s, c = i // 4, i % 4
             for way in (0, 1):
                 if s:
                     landed(p, way, s - 1, c)
                 hop(p, way, s, c).start()
+                if settle:
+                    hop(p - 1, way, s, c).wait_send()
 
     def finals(p):
         for way in (0, 1):
@@ -110,18 +110,13 @@
         for c in range(4):
             own(p, c).wait()
 
-    def inner(p, first, last):
-        def step(i, carry):
-            rows = pl.ds(pl.multiple_of(i * TILE, TILE), TILE)
-            left = halves(panel[p, :, :, rows].reshape(256, TILE))
-            term = product(left, (high[rows, :], low[rows, :])).reshape(part.shape[1:])
-            if first == 0:
-                part[p] = jnp.where(i == 0, term, part[p] + term)
-            else:
-                part[p] += term
-            return carry
-
-        lax.fori_loop(first, last, step, 0)
+    def inner(p, side):
+        rows = pl.ds(side * 16, 16)
+        total = 0.0
+        for i in range(blocks):
+            span = slice(i * TILE, (i + 1) * TILE)
+            total += product(halves(panel[p, rows, :, span].reshape(128, TILE)), (high[span, :], low[span, :]))
+        part[p, rows] = total.reshape(16, PIECE, -1)
 
     def turn(p, first, last):
         def step(i, carry):
@@ -160,12 +155,11 @@
             device_id=chip_device(k), device_id_type=MESH,
         )
 
+    far_first = sorted(range(1, 16), key=lambda k: -min(k % 4, 4 - k % 4) - min(k // 4, 4 - k // 4))
+
     def each(action):
-        def step(k, carry):
+        for k in far_first:
             action(k)
-            return carry
-
-        lax.fori_loop(1, 16, step, 0)
 
     def pair_sum(p):
         exchange(p).wait_recv()
@@ -182,107 +176,103 @@
         each(lambda k: shared(p, k).wait_recv())
         mine = sums.at[p, pl.ds(core * 16, 16)]
         to_twin(p, 1, mine, mine).start()
+        each(lambda k: share(p, k).wait_send())
 
     def coefficients(p):
         theirs = sums.at[p, pl.ds((1 - core) * 16, 16)]
-        to_twin(p, 1, theirs, theirs).wait_recv()
-        coef = jnp.dot(factors[p], sums[p].reshape(256, -1), precision=lax.Precision.HIGHEST, preferred_element_type=F32)
+        to_twin(p, 1, theirs, theirs).wait()
+        coef = product(halves(factors[p]), halves(sums[p].reshape(256, -1)))
         coef_high[...], coef_low[...] = halves(coef)
 
-    def update(p, last):
+    def update():
         def step(i, carry):
             rows = pl.ds(pl.multiple_of(i * TILE, TILE), TILE)
             fresh = field[rows, :] - product((plain_high[rows, :], plain_low[rows, :]), (coef_high[...], coef_low[...]))
             field[rows, :] = fresh
-            if last:
-                pltpu.make_async_copy(field.at[rows], out_ref.at[rows], out_sem.at[i]).start()
-            else:
-                high[rows, :], low[rows, :] = halves(fresh)
+            high[rows, :], low[rows, :] = halves(fresh)
             return carry
 
-        lax.fori_loop(0, blocks, step, 0)
-
-    def chain(p, slot, last):
+        lax.fori_loop(0, blocks, step, 0, unroll=4)
+
+    def chain(p, slot):
         finals(p)
-        inner(p, 0, 3)
+        inner(p, 1 - core)
+        exchange(p).start()
         slot(4, 5)
-        inner(p, 3, 6)
+        inner(p, core)
         slot(5, 6)
-        inner(p, 6, 8)
-        exchange(p).start()
-        slot(6, 7)
         pair_sum(p)
         each(lambda k: scatter(p, k).start())
-        for i in range(4):
-            turn(p, 2 * i, 2 * i + 2)
-            slot(7 + i, 8 + i)
+        exchange(p).wait_send()
+        turn(p, 0, 4)
+        slot(6, 7)
+        turn(p, 4, 8)
+        slot(7, 10)
         chip_sum(p)
         each(lambda k: share(p, k).start())
-        slot(11, 14)
-
-    def finish(p, last):
+        each(lambda k: scatter(p, k).wait_send())
+        slot(10, 14)
+
+    def finish(p):
         join(p)
         coefficients(p)
-        update(p, last)
-
+
+    slots(0, 0, 4, False)
+    load_field.wait()
+    lax.fori_loop(0, blocks, split, 0)
     load_factors.wait()
-    slots(0, 0, 14)
+    slots(0, 4, 14, False)
 
     def turn_of_panel(p, carry):
         slots(p, 0, 4)
 
         @pl.when(p > 1)
         def _():
-            finish(p - 2, False)
-
-        chain(p - 1, functools.partial(slots, p), False)
+            finish(p - 2)
+            update()
+
+        chain(p - 1, functools.partial(slots, p))
         return carry
 
     lax.fori_loop(1, panels, turn_of_panel, 0)
-    finish(panels - 2, False)
-    chain(panels - 1, lambda first, last: None, True)
-    finish(panels - 1, True)
-
-    def drain(p, carry):
-        for way in (0, 1):
-            for i in range(14):
-                hop(p, way, i // 4, i % 4).wait_send()
-        exchange(p).wait_send()
-        mine = sums.at[p, pl.ds(core * 16, 16)]
-        to_twin(p, 1, mine, mine).wait_send()
-        each(lambda k: scatter(p, k).wait_send())
-        each(lambda k: share(p, k).wait_send())
-        return carry
-
-    lax.fori_loop(0, panels, drain, 0)
-
-    def written(i, carry):
-        rows = pl.ds(pl.multiple_of(i * TILE, TILE), TILE)
-        pltpu.make_async_copy(field.at[rows], out_ref.at[rows], out_sem.at[i]).wait()
-        return carry
-
-    lax.fori_loop(0, blocks, written, 0)
+    finish(panels - 2)
+    update()
+
+    def settle_last(first, last):
+        for i in range(first - 4, last - 4 if last < 14 else 14):
+            for way in (0, 1):
+                hop(panels - 1, way, i // 4, i % 4).wait_send()
+
+    chain(panels - 1, settle_last)
+    finish(panels - 1)
+
+
+def last_update(field, plain_high, plain_low, coef_high, coef_low, out_ref, held, out_sem):
+    copies = []
+    for i in range(held.shape[0]):
+        rows = slice(i * TILE, (i + 1) * TILE)
+        held[i] = field[rows, :] - product((plain_high[rows, :], plain_low[rows, :]), (coef_high[...], coef_low[...]))
+        copies.append(pltpu.make_async_copy(held.at[i], out_ref.at[rows], out_sem.at[i]))
+        copies[i].start()
+    for copy in copies:
+        copy.wait()
 
 
 def body(eigvecs, reflectors, t_factors):
     rows, columns = eigvecs.shape
     panels, block = t_factors.shape[:2]
     dma, vmem = pltpu.SemaphoreType.DMA, pltpu.VMEM
-    return pl.pallas_call(
+    shapes = [((rows, columns), F32), ((rows, block), BF16), ((rows, block), BF16), ((block, columns), BF16), ((block, columns), BF16)]
+    parts = pl.pallas_call(
         kernel,
-        out_shape=jax.ShapeDtypeStruct((rows, columns), F32),
-        in_specs=[pl.BlockSpec(memory_space=pl.ANY)] * 3,
-        out_specs=pl.BlockSpec(memory_space=pl.ANY),
+        out_shape=[vmem(*shape) for shape in shapes],
+        in_specs=[pl.BlockSpec(memory_space=pltpu.HBM)] * 3,
+        out_specs=[pl.BlockSpec(memory_space=vmem)] * 5,
         scratch_shapes=[
             vmem((panels, block // PIECE, PIECE, rows), F32),
-            vmem((rows, columns), F32),
             vmem((rows, columns), BF16),
             vmem((rows, columns), BF16),
-            vmem((rows, block), BF16),
-            vmem((rows, block), BF16),
             vmem((panels, block, block), F32),
-            vmem((block, columns), BF16),
-            vmem((block, columns), BF16),
             vmem((panels, 32, 8, columns), F32),
             vmem((panels, 16, 8, columns), F32),
             vmem((panels, 16, 8, columns), F32),
@@ -298,11 +288,19 @@
             dma((panels, 2)),
             dma((panels, 4)),
             dma((2,)),
-            dma((rows // TILE,)),
         ],
-        compiler_params=pltpu.CompilerParams(collective_id=0, has_side_effects=True, vmem_limit_bytes=56 * 2**20),
-        cost_estimate=pl.CostEstimate(flops=13 * 10**9, bytes_accessed=10 * 2**20, transcendentals=0),
-    )(eigvecs, jnp.swapaxes(reflectors, 1, 2), t_factors)
+        compiler_params=pltpu.CompilerParams(collective_id=0, has_side_effects=True, vmem_limit_bytes=48 * 2**20),
+        cost_estimate=pl.CostEstimate(flops=12 * 10**9, bytes_accessed=6 * 2**20, transcendentals=0),
+    )(*(pltpu.with_memory_space_constraint(a, pltpu.HBM) for a in (eigvecs, jnp.swapaxes(reflectors, 1, 2), t_factors)))
+    return pl.pallas_call(
+        last_update,
+        out_shape=jax.ShapeDtypeStruct((rows, columns), F32),
+        in_specs=[pl.BlockSpec(memory_space=vmem)] * 5,
+        out_specs=pl.BlockSpec(memory_space=pl.ANY),
+        scratch_shapes=[vmem((rows // TILE, TILE, columns), F32), dma((rows // TILE,))],
+        compiler_params=pltpu.CompilerParams(vmem_limit_bytes=16 * 2**20),
+        cost_estimate=pl.CostEstimate(flops=2 * 10**9, bytes_accessed=4 * 2**20, transcendentals=0),
+    )(*parts)
 
 
 def solution(mesh):

time: 130 us -> 116 us (0.89)
  Pallas kernels: 125 us -> 116 us
  local copies, waits for them, and re-layouts: 4.64 us -> 0 us
    pallas_call x1 -> x2, Pallas kernels: 125 us -> 116 us  [the longest x1 113 us: body(): pl.pallas_call(kernel, out_shape=[vmem(*shape) for shape in shapes], in_s...]
    unnamed x1 -> x0, local copies, waits for them, and re-layouts: 4.64 us -> none
where the time goes in v2:
time: 116 us
  Pallas kernels  116 us (100%)
    pallas_call x1, Pallas kernels, body(): pl.pallas_call(kernel, out_shape=[vmem(*shape) for shape in shapes], in_s...  113 us
    pallas_call x1, Pallas kernels, body(): pl.pallas_call(last_update, out_shape=jax.ShapeDtypeStruct((rows, columns...  2.66 us

profile of v2, /device:TPU:1, one launch (start us, length us, event | category | flops | bytes accessed | tf_op | source)
XLA Modules:
  0.0 115.5 jit_solution(11933023615238357714)
XLA Ops:
  0.0 112.9 %shard_map.37 = (f32[2048,512]{1,0:T(8,128)S(1)}, bf16[2048,256]{1,0:T(8,128)(2,1)S(1)}, bf16[2048,256]{1,0:T(8,128)(2,1)S(1)}, bf16[256,512]{1,0:T(8,128)(2,1)S(1)}, bf16[256,512]{1,0:T(8,128)(2,1)S(1)}) custom-call(f32[2048,512]{1,0:T(8,128)} %field_in.1, f32[4,32,2048]{2,1,0:T(8,128)} %bitcast.1, f32[4,256,256]{2,1,0:T(8,128)} %factor_in.1), custom_call_target="tpu_custom_call" | custom-call | flops 12000000000 | bytes 6291456 | tf_op jit(solution)/shard_map/pallas_call | solution.py:266
  112.9 2.7 %shard_map.38 = f32[2048,512]{1,0:T(8,128)} custom-call(f32[2048,512]{1,0:T(8,128)S(1)} %get-tuple-element.10.field, bf16[2048,256]{1,0:T(8,128)(2,1)S(1)} %get-tuple-element.11.plain_high, bf16[2048,256]{1,0:T(8,128)(2,1)S(1)} %get-tuple-element.12.plain_low, bf16[256,512]{1,0:T(8,128)(2,1)S(1)} %get-tuple-element.13.coef_high, ...), custom_call_target="tpu_custom_call" | custom-call | flops 2000000000 | bytes 4194304 | tf_op jit(solution)/shard_map/pallas_call | solution.py:295

commit v3 on v2

--- a/solution.py
+++ b/solution.py
@@ -29,16 +29,16 @@
     field, plain_high, plain_low, coef_high, coef_low,
     panel, high, low, factors,
     part, pair, half, spread, sums,
-    z_send, z_recv, rs_send, rs_recv, ag_send, ag_recv, core_send, core_recv, own_sem, in_sem,
+    z_send, z_recv, rs_send, rs_recv, ag_send, ag_recv, core_send, core_recv, own_sem, in_sem, ready,
 ):
     row, z = lax.axis_index("rows"), lax.axis_index("cols")
-    core, chip = row % 2, row // 2
-    x, y = chip % 4, chip // 4
-    z_next = ((row, (z + 1) % 8), (row, (z + 7) % 8))
+    core, chip = lax.rem(row, 2), row // 2
+    x, y = lax.rem(chip, 4), chip // 4
+    z_next = ((row, lax.rem(z + 1, 8)), (row, lax.rem(z + 7, 8)))
     twin = (chip * 2 + 1 - core, z)
 
     def chip_at(k):
-        return ((y + k // 4) % 4) * 4 + (x + k % 4) % 4
+        return lax.rem(y + k // 4, 4) * 4 + lax.rem(x + k % 4, 4)
 
     def chip_device(k):
         return (chip_at(k) * 2 + core, z)
@@ -58,24 +58,27 @@
             own(p, c).start()
 
     barrier = pltpu.get_barrier_semaphore()
-    for device in (*z_next, twin):
+    beside = [chip_device(k) for k in (1, 3, 4, 12)]
+    for device in (*z_next, twin, *beside):
         pl.semaphore_signal(barrier, inc=1, device_id=device, device_id_type=MESH)
 
-    def greet(k, carry):
-        pl.semaphore_signal(barrier, inc=1, device_id=chip_device(k), device_id_type=MESH)
-        return carry
-
-    lax.fori_loop(1, 16, greet, 0)
+    def tell(stage):
+        for device in beside:
+            pl.semaphore_signal(ready.at[stage], inc=1, device_id=device, device_id_type=MESH)
+
+    def hear(stage):
+        pl.semaphore_wait(ready.at[stage], len(beside))
+
     def split(i, carry):
         rows = pl.ds(pl.multiple_of(i * TILE, TILE), TILE)
         high[rows, :], low[rows, :] = halves(field[rows, :])
         return carry
 
-    pl.semaphore_wait(barrier, 18)
+    pl.semaphore_wait(barrier, 7)
 
     def hop(p, way, s, c):
         c = c if way == 0 else 3 - c
-        owner = (z + 8 - s) % 8 if way == 0 else (z + s) % 8
+        owner = lax.rem(z + (8 - s if way == 0 else s), 8)
         source = refl_in.at[p, pl.ds(PIECE * c, PIECE)] if s == 0 else panel.at[p, owner * 4 + c]
         return pltpu.make_async_remote_copy(
             src_ref=source, dst_ref=panel.at[p, owner * 4 + c],
@@ -85,7 +88,7 @@
 
     def landed(p, way, s, c):
         c = c if way == 0 else 3 - c
-        owner = (z + 7 - s) % 8 if way == 0 else (z + 1 + s) % 8
+        owner = lax.rem(z + (7 - s if way == 0 else 1 + s), 8)
         place = panel.at[p, owner * 4 + c]
         pltpu.make_async_remote_copy(
             src_ref=place, dst_ref=place,
@@ -149,7 +152,7 @@
         )
 
     def shared(p, k):
-        theirs = sums.at[p, core * 16 + ((y + 4 - k // 4) % 4) * 4 + (x + 4 - k % 4) % 4]
+        theirs = sums.at[p, core * 16 + chip_at((4 - k // 4) % 4 * 4 + (4 - k % 4) % 4)]
         return pltpu.make_async_remote_copy(
             src_ref=theirs, dst_ref=theirs, send_sem=ag_send.at[p, k], recv_sem=ag_recv.at[p, k],
             device_id=chip_device(k), device_id_type=MESH,
@@ -179,10 +182,14 @@
         each(lambda k: share(p, k).wait_send())
 
     def coefficients(p):
+        def term(side):
+            rows, columns = pl.ds(side * 16, 16), pl.ds(pl.multiple_of(side * 128, 128), 128)
+            return product(halves(factors[p, :, columns]), halves(sums[p, rows].reshape(128, -1)))
+
+        coef = term(core)
         theirs = sums.at[p, pl.ds((1 - core) * 16, 16)]
         to_twin(p, 1, theirs, theirs).wait()
-        coef = product(halves(factors[p]), halves(sums[p].reshape(256, -1)))
-        coef_high[...], coef_low[...] = halves(coef)
+        coef_high[...], coef_low[...] = halves(coef + term(1 - core))
 
     def update():
         def step(i, carry):
@@ -221,7 +228,11 @@
     load_field.wait()
     lax.fori_loop(0, blocks, split, 0)
     load_factors.wait()
-    slots(0, 4, 14, False)
+    for stage in range(3):
+        tell(stage)
+        slots(0, 4 + 2 * stage, 6 + 2 * stage, False)
+        hear(stage)
+    slots(0, 10, 14, False)
 
     def turn_of_panel(p, carry):
         slots(p, 0, 4)
@@ -288,6 +299,7 @@
             dma((panels, 2)),
             dma((panels, 4)),
             dma((2,)),
+            pltpu.SemaphoreType.REGULAR((3,)),
         ],
         compiler_params=pltpu.CompilerParams(collective_id=0, has_side_effects=True, vmem_limit_bytes=48 * 2**20),
         cost_estimate=pl.CostEstimate(flops=12 * 10**9, bytes_accessed=6 * 2**20, transcendentals=0),

time: 116 us -> 114 us (0.983)
  Pallas kernels: 116 us -> 113 us
    pallas_call x1, Pallas kernels: 113 us -> 111 us  [body(): pl.pallas_call(kernel, out_shape=[vmem(*shape) for shape in shapes], in_s...]
where the time goes in v3:
time: 114 us; the launch traced here: 113 us
  Pallas kernels  113 us (99%)
    pallas_call x1, Pallas kernels, body(): pl.pallas_call(kernel, out_shape=[vmem(*shape) for shape in shapes], in_s...  111 us
    pallas_call x1, Pallas kernels, body(): pl.pallas_call(last_update, out_shape=jax.ShapeDtypeStruct((rows, columns...  2.66 us

profile of v3, /device:TPU:1, one launch (start us, length us, event | category | flops | bytes accessed | tf_op | source)
XLA Modules:
  0.0 113.4 jit_solution(17314185267219666178)
XLA Ops:
  0.0 110.8 %shard_map.37 = (f32[2048,512]{1,0:T(8,128)S(1)}, bf16[2048,256]{1,0:T(8,128)(2,1)S(1)}, bf16[2048,256]{1,0:T(8,128)(2,1)S(1)}, bf16[256,512]{1,0:T(8,128)(2,1)S(1)}, bf16[256,512]{1,0:T(8,128)(2,1)S(1)}) custom-call(f32[2048,512]{1,0:T(8,128)} %field_in.1, f32[4,32,2048]{2,1,0:T(8,128)} %bitcast.1, f32[4,256,256]{2,1,0:T(8,128)} %factor_in.1), custom_call_target="tpu_custom_call" | custom-call | flops 12000000000 | bytes 6291456 | tf_op jit(solution)/shard_map/pallas_call | solution.py:277
  110.8 2.7 %shard_map.38 = f32[2048,512]{1,0:T(8,128)} custom-call(f32[2048,512]{1,0:T(8,128)S(1)} %get-tuple-element.10.field, bf16[2048,256]{1,0:T(8,128)(2,1)S(1)} %get-tuple-element.11.plain_high, bf16[2048,256]{1,0:T(8,128)(2,1)S(1)} %get-tuple-element.12.plain_low, bf16[256,512]{1,0:T(8,128)(2,1)S(1)} %get-tuple-element.13.coef_high, ...), custom_call_target="tpu_custom_call" | custom-call | flops 2000000000 | bytes 4194304 | tf_op jit(solution)/shard_map/pallas_call | solution.py:307

commit v4 on v3

--- a/solution.py
+++ b/solution.py
@@ -29,7 +29,7 @@
     field, plain_high, plain_low, coef_high, coef_low,
     panel, high, low, factors,
     part, pair, half, spread, sums,
-    z_send, z_recv, rs_send, rs_recv, ag_send, ag_recv, core_send, core_recv, own_sem, in_sem, ready,
+    z_send, z_recv, rs_send, rs_recv, ag_send, ag_recv, core_send, core_recv, in_sem, ready,
 ):
     row, z = lax.axis_index("rows"), lax.axis_index("cols")
     core, chip = lax.rem(row, 2), row // 2
@@ -45,18 +45,6 @@
 
     panels, blocks = panel.shape[0], field.shape[0] // TILE
 
-    load_field = pltpu.make_async_copy(field_in, field, in_sem.at[0])
-    load_factors = pltpu.make_async_copy(factor_in, factors, in_sem.at[1])
-    load_field.start()
-    load_factors.start()
-
-    def own(p, c):
-        return pltpu.make_async_copy(refl_in.at[p, pl.ds(PIECE * c, PIECE)], panel.at[p, z * 4 + c], own_sem.at[p, c])
-
-    for p in range(panels):
-        for c in range(4):
-            own(p, c).start()
-
     barrier = pltpu.get_barrier_semaphore()
     beside = [chip_device(k) for k in (1, 3, 4, 12)]
     for device in (*z_next, twin, *beside):
@@ -74,12 +62,17 @@
         high[rows, :], low[rows, :] = halves(field[rows, :])
         return carry
 
+
+    load_field = pltpu.make_async_copy(field_in, field, in_sem.at[0])
+    load_factors = pltpu.make_async_copy(factor_in, factors, in_sem.at[1])
+    load_own = pltpu.make_async_copy(refl_in, panel.at[:, pl.ds(z * 4, 4)], in_sem.at[2])
+    load_field.start()
     pl.semaphore_wait(barrier, 7)
 
     def hop(p, way, s, c):
         c = c if way == 0 else 3 - c
         owner = lax.rem(z + (8 - s if way == 0 else s), 8)
-        source = refl_in.at[p, pl.ds(PIECE * c, PIECE)] if s == 0 else panel.at[p, owner * 4 + c]
+        source = refl_in.at[p, c] if s == 0 else panel.at[p, owner * 4 + c]
         return pltpu.make_async_remote_copy(
             src_ref=source, dst_ref=panel.at[p, owner * 4 + c],
             send_sem=z_send.at[p, way, s, c], recv_sem=z_recv.at[p, way, s, c],
@@ -110,8 +103,6 @@
         for way in (0, 1):
             for s, c in ((2, 2), (2, 3), (3, 0), (3, 1)):
                 landed(p, way, s, c)
-        for c in range(4):
-            own(p, c).wait()
 
     def inner(p, side):
         rows = pl.ds(side * 16, 16)
@@ -140,22 +131,27 @@
 
     def scatter(p, k):
         return pltpu.make_async_remote_copy(
-            src_ref=half.at[p, chip_at(k)], dst_ref=spread.at[p, k], send_sem=rs_send.at[p, k], recv_sem=rs_recv.at[p, k],
+            src_ref=half.at[p, chip_at(k)], dst_ref=spread.at[p, k - 1], send_sem=rs_send.at[p], recv_sem=rs_recv.at[p],
             device_id=chip_device(k), device_id_type=MESH,
         )
 
     def share(p, k):
         mine = sums.at[p, core * 16 + chip]
         return pltpu.make_async_remote_copy(
-            src_ref=mine, dst_ref=mine, send_sem=ag_send.at[p, k], recv_sem=ag_recv.at[p, k],
+            src_ref=mine, dst_ref=mine, send_sem=ag_send.at[p], recv_sem=ag_recv.at[p],
             device_id=chip_device(k), device_id_type=MESH,
         )
 
-    def shared(p, k):
-        theirs = sums.at[p, core * 16 + chip_at((4 - k // 4) % 4 * 4 + (4 - k % 4) % 4)]
-        return pltpu.make_async_remote_copy(
-            src_ref=theirs, dst_ref=theirs, send_sem=ag_send.at[p, k], recv_sem=ag_recv.at[p, k],
-            device_id=chip_device(k), device_id_type=MESH,
+    def all_scattered(p):
+        whole = spread.at[p]
+        return pltpu.make_async_remote_copy(
+            src_ref=whole, dst_ref=whole, send_sem=rs_send.at[p], recv_sem=rs_recv.at[p], device_id=twin, device_id_type=MESH
+        )
+
+    def all_shared(p):
+        whole = sums.at[p, pl.ds(0, 15)]
+        return pltpu.make_async_remote_copy(
+            src_ref=whole, dst_ref=whole, send_sem=ag_send.at[p], recv_sem=ag_recv.at[p], device_id=twin, device_id_type=MESH
         )
 
     far_first = sorted(range(1, 16), key=lambda k: -min(k % 4, 4 - k % 4) - min(k // 4, 4 - k // 4))
@@ -169,17 +165,17 @@
         half[p] = part[p, pl.ds(core * 16, 16)] + pair[p]
 
     def chip_sum(p):
-        each(lambda k: scatter(p, k).wait_recv())
+        all_scattered(p).wait_recv()
         total = half[p, chip]
-        for k in range(1, 16):
+        for k in range(15):
             total = total + spread[p, k]
         sums[p, core * 16 + chip] = total
 
     def join(p):
-        each(lambda k: shared(p, k).wait_recv())
+        all_shared(p).wait_recv()
         mine = sums.at[p, pl.ds(core * 16, 16)]
         to_twin(p, 1, mine, mine).start()
-        each(lambda k: share(p, k).wait_send())
+        all_shared(p).wait_send()
 
     def coefficients(p):
         def term(side):
@@ -217,7 +213,7 @@
         slot(7, 10)
         chip_sum(p)
         each(lambda k: share(p, k).start())
-        each(lambda k: scatter(p, k).wait_send())
+        all_scattered(p).wait_send()
         slot(10, 14)
 
     def finish(p):
@@ -225,6 +221,8 @@
         coefficients(p)
 
     slots(0, 0, 4, False)
+    load_own.start()
+    load_factors.start()
     load_field.wait()
     lax.fori_loop(0, blocks, split, 0)
     load_factors.wait()
@@ -233,6 +231,7 @@
         slots(0, 4 + 2 * stage, 6 + 2 * stage, False)
         hear(stage)
     slots(0, 10, 14, False)
+    load_own.wait()
 
     def turn_of_panel(p, carry):
         slots(p, 0, 4)
@@ -274,6 +273,7 @@
     panels, block = t_factors.shape[:2]
     dma, vmem = pltpu.SemaphoreType.DMA, pltpu.VMEM
     shapes = [((rows, columns), F32), ((rows, block), BF16), ((rows, block), BF16), ((block, columns), BF16), ((block, columns), BF16)]
+    own = jnp.swapaxes(reflectors, 1, 2).reshape(panels, -1, PIECE, rows)
     parts = pl.pallas_call(
         kernel,
         out_shape=[vmem(*shape) for shape in shapes],
@@ -287,23 +287,22 @@
             vmem((panels, 32, 8, columns), F32),
             vmem((panels, 16, 8, columns), F32),
             vmem((panels, 16, 8, columns), F32),
-            vmem((panels, 16, 8, columns), F32),
+            vmem((panels, 15, 8, columns), F32),
             vmem((panels, 32, 8, columns), F32),
             dma((panels, 2, 4, 4)),
             dma((panels, 2, 4, 4)),
-            dma((panels, 16)),
-            dma((panels, 16)),
-            dma((panels, 16)),
-            dma((panels, 16)),
+            dma((panels,)),
+            dma((panels,)),
+            dma((panels,)),
+            dma((panels,)),
             dma((panels, 2)),
             dma((panels, 2)),
-            dma((panels, 4)),
-            dma((2,)),
+            dma((3,)),
             pltpu.SemaphoreType.REGULAR((3,)),
         ],
         compiler_params=pltpu.CompilerParams(collective_id=0, has_side_effects=True, vmem_limit_bytes=48 * 2**20),
         cost_estimate=pl.CostEstimate(flops=12 * 10**9, bytes_accessed=6 * 2**20, transcendentals=0),
-    )(*(pltpu.with_memory_space_constraint(a, pltpu.HBM) for a in (eigvecs, jnp.swapaxes(reflectors, 1, 2), t_factors)))
+    )(*(pltpu.with_memory_space_constraint(a, pltpu.HBM) for a in (eigvecs, own, t_factors)))
     return pl.pallas_call(
         last_update,
         out_shape=jax.ShapeDtypeStruct((rows, columns), F32),

time: 114 us -> 111 us (0.974)
  Pallas kernels: 113 us -> 111 us
    pallas_call x1, Pallas kernels: 111 us -> 108 us  [body(): pl.pallas_call(kernel, out_shape=[vmem(*shape) for shape in shapes], in_s...]
where the time goes in v4:
time: 111 us
  Pallas kernels  111 us (100%)
    pallas_call x1, Pallas kernels, body(): pl.pallas_call(kernel, out_shape=[vmem(*shape) for shape in shapes], in_s...  108 us
    pallas_call x1, Pallas kernels, body(): pl.pallas_call(last_update, out_shape=jax.ShapeDtypeStruct((rows, columns...  2.66 us

profile of v4, /device:TPU:1, one launch (start us, length us, event | category | flops | bytes accessed | tf_op | source)
XLA Modules:
  0.0 111.1 jit_solution(6301773165536100720)
XLA Ops:
  0.0 108.4 %shard_map.37 = (f32[2048,512]{1,0:T(8,128)S(1)}, bf16[2048,256]{1,0:T(8,128)(2,1)S(1)}, bf16[2048,256]{1,0:T(8,128)(2,1)S(1)}, bf16[256,512]{1,0:T(8,128)(2,1)S(1)}, bf16[256,512]{1,0:T(8,128)(2,1)S(1)}) custom-call(f32[2048,512]{1,0:T(8,128)} %field_in.1, f32[4,4,8,2048]{3,2,1,0:T(8,128)} %bitcast.3, f32[4,256,256]{2,1,0:T(8,128)} %factor_in.1), custom_call_target="tpu_custom_call" | custom-call | flops 12000000000 | bytes 6291456 | tf_op jit(solution)/shard_map/pallas_call | solution.py:277
  108.4 2.7 %shard_map.38 = f32[2048,512]{1,0:T(8,128)} custom-call(f32[2048,512]{1,0:T(8,128)S(1)} %get-tuple-element.10.field, bf16[2048,256]{1,0:T(8,128)(2,1)S(1)} %get-tuple-element.11.plain_high, bf16[2048,256]{1,0:T(8,128)(2,1)S(1)} %get-tuple-element.12.plain_low, bf16[256,512]{1,0:T(8,128)(2,1)S(1)} %get-tuple-element.13.coef_high, ...), custom_call_target="tpu_custom_call" | custom-call | flops 2000000000 | bytes 4194304 | tf_op jit(solution)/shard_map/pallas_call | solution.py:306

commit v5 on v4

--- a/solution.py
+++ b/solution.py
@@ -69,40 +69,43 @@
     load_field.start()
     pl.semaphore_wait(barrier, 7)
 
+    def move(p, way, owner, c, step, source=None):
+        piece = c if way == 0 else 3 - c
+        place = panel.at[p, lax.rem(owner, 8) * 4 + piece]
+        return pltpu.make_async_remote_copy(
+            src_ref=place if source is None else source.at[p, piece], dst_ref=place, send_sem=z_send.at[p, way],
+            recv_sem=z_recv.at[p, way, step * 4 + c if step < 2 or (step == 2 and c < 2) else 10],
+            device_id=z_next[way], device_id_type=MESH,
+        )
+
     def hop(p, way, s, c):
-        c = c if way == 0 else 3 - c
-        owner = lax.rem(z + (8 - s if way == 0 else s), 8)
-        source = refl_in.at[p, c] if s == 0 else panel.at[p, owner * 4 + c]
-        return pltpu.make_async_remote_copy(
-            src_ref=source, dst_ref=panel.at[p, owner * 4 + c],
-            send_sem=z_send.at[p, way, s, c], recv_sem=z_recv.at[p, way, s, c],
+        return move(p, way, z + (8 - s if way == 0 else s), c, s, refl_in if s == 0 else None)
+
+    def landed(p, way, s, c):
+        move(p, way, z + (7 - s if way == 0 else 1 + s), c, s).wait_recv()
+
+    def many(p, way, count):
+        places = panel.at[p, pl.ds(0, count)]
+        return pltpu.make_async_remote_copy(
+            src_ref=places, dst_ref=places, send_sem=z_send.at[p, way], recv_sem=z_recv.at[p, way, 10],
             device_id=z_next[way], device_id_type=MESH,
         )
 
-    def landed(p, way, s, c):
-        c = c if way == 0 else 3 - c
-        owner = lax.rem(z + (7 - s if way == 0 else 1 + s), 8)
-        place = panel.at[p, owner * 4 + c]
-        pltpu.make_async_remote_copy(
-            src_ref=place, dst_ref=place,
-            send_sem=z_send.at[p, way, s, c], recv_sem=z_recv.at[p, way, s, c],
-            device_id=z_next[way], device_id_type=MESH,
-        ).wait_recv()
-
-    def slots(p, first, last, settle=True):
+    def slots(p, first, last):
         for i in range(first, last):
             s, c = i // 4, i % 4
             for way in (0, 1):
                 if s:
                     landed(p, way, s - 1, c)
                 hop(p, way, s, c).start()
-                if settle:
-                    hop(p - 1, way, s, c).wait_send()
+
+    def sent(p):
+        for way in (0, 1):
+            many(p, way, 14).wait_send()
 
     def finals(p):
         for way in (0, 1):
-            for s, c in ((2, 2), (2, 3), (3, 0), (3, 1)):
-                landed(p, way, s, c)
+            many(p, way, 4).wait_recv()
 
     def inner(p, side):
         rows = pl.ds(side * 16, 16)
@@ -214,13 +217,14 @@
         chip_sum(p)
         each(lambda k: share(p, k).start())
         all_scattered(p).wait_send()
+        sent(p)
         slot(10, 14)
 
     def finish(p):
         join(p)
         coefficients(p)
 
-    slots(0, 0, 4, False)
+    slots(0, 0, 4)
     load_own.start()
     load_factors.start()
     load_field.wait()
@@ -228,9 +232,9 @@
     load_factors.wait()
     for stage in range(3):
         tell(stage)
-        slots(0, 4 + 2 * stage, 6 + 2 * stage, False)
+        slots(0, 4 + 2 * stage, 6 + 2 * stage)
         hear(stage)
-    slots(0, 10, 14, False)
+    slots(0, 10, 14)
     load_own.wait()
 
     def turn_of_panel(p, carry):
@@ -248,12 +252,7 @@
     finish(panels - 2)
     update()
 
-    def settle_last(first, last):
-        for i in range(first - 4, last - 4 if last < 14 else 14):
-            for way in (0, 1):
-                hop(panels - 1, way, i // 4, i % 4).wait_send()
-
-    chain(panels - 1, settle_last)
+    chain(panels - 1, lambda first, last: None)
     finish(panels - 1)
 
 
@@ -289,8 +288,8 @@
             vmem((panels, 16, 8, columns), F32),
             vmem((panels, 15, 8, columns), F32),
             vmem((panels, 32, 8, columns), F32),
-            dma((panels, 2, 4, 4)),
-            dma((panels, 2, 4, 4)),
+            dma((panels, 2)),
+            dma((panels, 2, 11)),
             dma((panels,)),
             dma((panels,)),
             dma((panels,)),

time: 111 us -> 110 us (level)
    pallas_call x1, Pallas kernels: 108 us -> 107 us  [body(): pl.pallas_call(kernel, out_shape=[vmem(*shape) for shape in shapes], in_s...]
where the time goes in v5:
time: 110 us
  Pallas kernels  110 us (100%)
    pallas_call x1, Pallas kernels, body(): pl.pallas_call(kernel, out_shape=[vmem(*shape) for shape in shapes], in_s...  107 us
    pallas_call x1, Pallas kernels, body(): pl.pallas_call(last_update, out_shape=jax.ShapeDtypeStruct((rows, columns...  2.66 us

profile of v5, /device:TPU:1, one launch (start us, length us, event | category | flops | bytes accessed | tf_op | source)
XLA Modules:
  0.0 109.7 jit_solution(17353686660629263497)
XLA Ops:
  0.0 107.0 %shard_map.37 = (f32[2048,512]{1,0:T(8,128)S(1)}, bf16[2048,256]{1,0:T(8,128)(2,1)S(1)}, bf16[2048,256]{1,0:T(8,128)(2,1)S(1)}, bf16[256,512]{1,0:T(8,128)(2,1)S(1)}, bf16[256,512]{1,0:T(8,128)(2,1)S(1)}) custom-call(f32[2048,512]{1,0:T(8,128)} %field_in.1, f32[4,4,8,2048]{3,2,1,0:T(8,128)} %bitcast.3, f32[4,256,256]{2,1,0:T(8,128)} %factor_in.1), custom_call_target="tpu_custom_call" | custom-call | flops 12000000000 | bytes 6291456 | tf_op jit(solution)/shard_map/pallas_call | solution.py:276
  107.0 2.7 %shard_map.38 = f32[2048,512]{1,0:T(8,128)} custom-call(f32[2048,512]{1,0:T(8,128)S(1)} %get-tuple-element.10.field, bf16[2048,256]{1,0:T(8,128)(2,1)S(1)} %get-tuple-element.11.plain_high, bf16[2048,256]{1,0:T(8,128)(2,1)S(1)} %get-tuple-element.12.plain_low, bf16[256,512]{1,0:T(8,128)(2,1)S(1)} %get-tuple-element.13.coef_high, ...), custom_call_target="tpu_custom_call" | custom-call | flops 2000000000 | bytes 4194304 | tf_op jit(solution)/shard_map/pallas_call | solution.py:305

commit v6 on v5

--- a/solution.py
+++ b/solution.py
@@ -115,13 +115,16 @@
             total += product(halves(panel[p, rows, :, span].reshape(128, TILE)), (high[span, :], low[span, :]))
         part[p, rows] = total.reshape(16, PIECE, -1)
 
-    def turn(p, first, last):
+    def fold(p, first, last):
+        factor = halves(factors[p])
+
         def step(i, carry):
             rows = pl.ds(pl.multiple_of(i * TILE, TILE), TILE)
-            plain_high[rows, :], plain_low[rows, :] = halves(panel[p, :, :, rows].reshape(256, TILE).T)
+            plain = halves(panel[p, :, :, rows].reshape(256, TILE).T)
+            plain_high[rows, :], plain_low[rows, :] = halves(product(plain, factor))
             return carry
 
-        lax.fori_loop(first, last, step, 0)
+        lax.fori_loop(first, last, step, 0, unroll=2)
 
     def to_twin(p, which, source, target):
         return pltpu.make_async_remote_copy(
@@ -181,14 +184,14 @@
         all_shared(p).wait_send()
 
     def coefficients(p):
-        def term(side):
-            rows, columns = pl.ds(side * 16, 16), pl.ds(pl.multiple_of(side * 128, 128), 128)
-            return product(halves(factors[p, :, columns]), halves(sums[p, rows].reshape(128, -1)))
-
-        coef = term(core)
+        def take(side):
+            rows = pl.ds(pl.multiple_of(side * 128, 128), 128)
+            coef_high[rows, :], coef_low[rows, :] = halves(sums[p, pl.ds(side * 16, 16)].reshape(128, -1))
+
+        take(core)
         theirs = sums.at[p, pl.ds((1 - core) * 16, 16)]
         to_twin(p, 1, theirs, theirs).wait()
-        coef_high[...], coef_low[...] = halves(coef + term(1 - core))
+        take(1 - core)
 
     def update():
         def step(i, carry):
@@ -210,9 +213,9 @@
         pair_sum(p)
         each(lambda k: scatter(p, k).start())
         exchange(p).wait_send()
-        turn(p, 0, 4)
+        fold(p, 0, 4)
         slot(6, 7)
-        turn(p, 4, 8)
+        fold(p, 4, 8)
         slot(7, 10)
         chip_sum(p)
         each(lambda k: share(p, k).start())

time: 110 us -> 109 us (level)
  no operation moved by 1% of the time
where the time goes in v6:
time: 109 us
  Pallas kernels  109 us (100%)
    pallas_call x1, Pallas kernels, body(): pl.pallas_call(kernel, out_shape=[vmem(*shape) for shape in shapes], in_s...  107 us
    pallas_call x1, Pallas kernels, body(): pl.pallas_call(last_update, out_shape=jax.ShapeDtypeStruct((rows, columns...  2.66 us

profile of v6, /device:TPU:1, one launch (start us, length us, event | category | flops | bytes accessed | tf_op | source)
XLA Modules:
  0.0 109.4 jit_solution(109554444454836133)
XLA Ops:
  0.0 106.7 %shard_map.37 = (f32[2048,512]{1,0:T(8,128)S(1)}, bf16[2048,256]{1,0:T(8,128)(2,1)S(1)}, bf16[2048,256]{1,0:T(8,128)(2,1)S(1)}, bf16[256,512]{1,0:T(8,128)(2,1)S(1)}, bf16[256,512]{1,0:T(8,128)(2,1)S(1)}) custom-call(f32[2048,512]{1,0:T(8,128)} %field_in.1, f32[4,4,8,2048]{3,2,1,0:T(8,128)} %bitcast.3, f32[4,256,256]{2,1,0:T(8,128)} %factor_in.1), custom_call_target="tpu_custom_call" | custom-call | flops 12000000000 | bytes 6291456 | tf_op jit(solution)/shard_map/pallas_call | solution.py:279
  106.7 2.7 %shard_map.38 = f32[2048,512]{1,0:T(8,128)} custom-call(f32[2048,512]{1,0:T(8,128)S(1)} %get-tuple-element.10.field, bf16[2048,256]{1,0:T(8,128)(2,1)S(1)} %get-tuple-element.11.plain_high, bf16[2048,256]{1,0:T(8,128)(2,1)S(1)} %get-tuple-element.12.plain_low, bf16[256,512]{1,0:T(8,128)(2,1)S(1)} %get-tuple-element.13.coef_high, ...), custom_call_target="tpu_custom_call" | custom-call | flops 2000000000 | bytes 4194304 | tf_op jit(solution)/shard_map/pallas_call | solution.py:308

commit v7 on v6

--- a/solution.py
+++ b/solution.py
@@ -24,10 +24,15 @@
     return dot(left_high, right_high) + (dot(left_high, right_low) + dot(left_low, right_high))
 
 
+def narrow(both, twice, single):
+    dot = functools.partial(jnp.dot, preferred_element_type=F32)
+    return dot(both, twice) + dot(both[:, :128], single)
+
+
 def kernel(
     field_in, refl_in, factor_in,
-    field, plain_high, plain_low, coef_high, coef_low,
-    panel, high, low, factors,
+    field, out_both, out_twice, out_single,
+    panel, high, low, factors, plain_high, plain_low, coef_high, coef_low, own_both,
     part, pair, half, spread, sums,
     z_send, z_recv, rs_send, rs_recv, ag_send, ag_recv, core_send, core_recv, in_sem, ready,
 ):
@@ -115,13 +120,18 @@
             total += product(halves(panel[p, rows, :, span].reshape(128, TILE)), (high[span, :], low[span, :]))
         part[p, rows] = total.reshape(16, PIECE, -1)
 
-    def fold(p, first, last):
+    def fold(p, first, last, apart):
         factor = halves(factors[p])
 
         def step(i, carry):
             rows = pl.ds(pl.multiple_of(i * TILE, TILE), TILE)
             plain = halves(panel[p, :, :, rows].reshape(256, TILE).T)
             plain_high[rows, :], plain_low[rows, :] = halves(product(plain, factor))
+            if apart:
+                for side, both in ((core, own_both), (1 - core, out_both)):
+                    columns = pl.ds(pl.multiple_of(side * 128, 128), 128)
+                    both[rows, :128] = plain_high[rows, columns]
+                    both[rows, 128:] = plain_low[rows, columns]
             return carry
 
         lax.fori_loop(first, last, step, 0, unroll=2)
@@ -203,7 +213,7 @@
 
         lax.fori_loop(0, blocks, step, 0, unroll=4)
 
-    def chain(p, slot):
+    def chain(p, slot, last=False):
         finals(p)
         inner(p, 1 - core)
         exchange(p).start()
@@ -213,9 +223,9 @@
         pair_sum(p)
         each(lambda k: scatter(p, k).start())
         exchange(p).wait_send()
-        fold(p, 0, 4)
+        fold(p, 0, 4, last)
         slot(6, 7)
-        fold(p, 4, 8)
+        fold(p, 4, 8, last)
         slot(7, 10)
         chip_sum(p)
         each(lambda k: share(p, k).start())
@@ -255,15 +265,27 @@
     finish(panels - 2)
     update()
 
-    chain(panels - 1, lambda first, last: None)
-    finish(panels - 1)
-
-
-def last_update(field, plain_high, plain_low, coef_high, coef_low, out_ref, held, out_sem):
+
+    def coefs(side):
+        coef_high, coef_low = halves(sums[panels - 1, pl.ds(side * 16, 16)].reshape(128, -1))
+        return jnp.concatenate([coef_high, coef_high], 0), coef_low
+
+    chain(panels - 1, lambda first, last: None, True)
+    join(panels - 1)
+    twice, single = coefs(core)
+    for i in range(blocks):
+        rows = slice(i * TILE, (i + 1) * TILE)
+        field[rows, :] -= narrow(own_both[rows, :], twice, single)
+    theirs = sums.at[panels - 1, pl.ds((1 - core) * 16, 16)]
+    to_twin(panels - 1, 1, theirs, theirs).wait()
+    out_twice[...], out_single[...] = coefs(1 - core)
+
+
+def last_update(field, both, twice, single, out_ref, held, out_sem):
     copies = []
     for i in range(held.shape[0]):
         rows = slice(i * TILE, (i + 1) * TILE)
-        held[i] = field[rows, :] - product((plain_high[rows, :], plain_low[rows, :]), (coef_high[...], coef_low[...]))
+        held[i] = field[rows, :] - narrow(both[rows, :], twice[...], single[...])
         copies.append(pltpu.make_async_copy(held.at[i], out_ref.at[rows], out_sem.at[i]))
         copies[i].start()
     for copy in copies:
@@ -274,18 +296,23 @@
     rows, columns = eigvecs.shape
     panels, block = t_factors.shape[:2]
     dma, vmem = pltpu.SemaphoreType.DMA, pltpu.VMEM
-    shapes = [((rows, columns), F32), ((rows, block), BF16), ((rows, block), BF16), ((block, columns), BF16), ((block, columns), BF16)]
+    shapes = [((rows, columns), F32), ((rows, block), BF16), ((block, columns), BF16), ((block // 2, columns), BF16)]
     own = jnp.swapaxes(reflectors, 1, 2).reshape(panels, -1, PIECE, rows)
     parts = pl.pallas_call(
         kernel,
         out_shape=[vmem(*shape) for shape in shapes],
         in_specs=[pl.BlockSpec(memory_space=pltpu.HBM)] * 3,
-        out_specs=[pl.BlockSpec(memory_space=vmem)] * 5,
+        out_specs=[pl.BlockSpec(memory_space=vmem)] * 4,
         scratch_shapes=[
             vmem((panels, block // PIECE, PIECE, rows), F32),
             vmem((rows, columns), BF16),
             vmem((rows, columns), BF16),
             vmem((panels, block, block), F32),
+            vmem((rows, block), BF16),
+            vmem((rows, block), BF16),
+            vmem((block, columns), BF16),
+            vmem((block, columns), BF16),
+            vmem((rows, block), BF16),
             vmem((panels, 32, 8, columns), F32),
             vmem((panels, 16, 8, columns), F32),
             vmem((panels, 16, 8, columns), F32),
@@ -308,7 +335,7 @@
     return pl.pallas_call(
         last_update,
         out_shape=jax.ShapeDtypeStruct((rows, columns), F32),
-        in_specs=[pl.BlockSpec(memory_space=vmem)] * 5,
+        in_specs=[pl.BlockSpec(memory_space=vmem)] * 4,
         out_specs=pl.BlockSpec(memory_space=pl.ANY),
         scratch_shapes=[vmem((rows // TILE, TILE, columns), F32), dma((rows // TILE,))],
         compiler_params=pltpu.CompilerParams(vmem_limit_bytes=16 * 2**20),

time: 109 us -> 109 us (level)
  no operation moved by 1% of the time
where the time goes in v7:
time: 109 us
  Pallas kernels  109 us (100%)
    pallas_call x1, Pallas kernels, body(): pl.pallas_call(kernel, out_shape=[vmem(*shape) for shape in shapes], in_s...  107 us
    pallas_call x1, Pallas kernels, body(): pl.pallas_call(last_update, out_shape=jax.ShapeDtypeStruct((rows, columns...  2.36 us

profile of v7, /device:TPU:1, one launch (start us, length us, event | category | flops | bytes accessed | tf_op | source)
XLA Modules:
  0.0 109.1 jit_solution(6909541421534153034)
XLA Ops:
  0.0 106.7 %shard_map.37 = (f32[2048,512]{1,0:T(8,128)S(1)}, bf16[2048,256]{1,0:T(8,128)(2,1)S(1)}, bf16[256,512]{1,0:T(8,128)(2,1)S(1)}, bf16[128,512]{1,0:T(8,128)(2,1)S(1)}) custom-call(f32[2048,512]{1,0:T(8,128)} %field_in.1, f32[4,4,8,2048]{3,2,1,0:T(8,128)} %bitcast.3, f32[4,256,256]{2,1,0:T(8,128)} %factor_in.1), custom_call_target="tpu_custom_call" | custom-call | flops 12000000000 | bytes 6291456 | tf_op jit(solution)/shard_map/pallas_call | solution.py:301
  106.7 2.4 %shard_map.38 = f32[2048,512]{1,0:T(8,128)} custom-call(f32[2048,512]{1,0:T(8,128)S(1)} %get-tuple-element.9.field, bf16[2048,256]{1,0:T(8,128)(2,1)S(1)} %get-tuple-element.10.both, bf16[256,512]{1,0:T(8,128)(2,1)S(1)} %get-tuple-element.11.twice, bf16[128,512]{1,0:T(8,128)(2,1)S(1)} %get-tuple-element.12.single), custom_call_target="tpu_custom_call" | custom-call | flops 2000000000 | bytes 4194304 | tf_op jit(solution)/shard_map/pallas_call | solution.py:335

commit v8 on v6

--- a/solution.py
+++ b/solution.py
@@ -201,7 +201,7 @@
             high[rows, :], low[rows, :] = halves(fresh)
             return carry
 
-        lax.fori_loop(0, blocks, step, 0, unroll=4)
+        lax.fori_loop(0, blocks, step, 0, unroll=8)
 
     def chain(p, slot):
         finals(p)

time: 109 us -> 109 us (level)
  no operation moved by 1% of the time
where the time goes in v8:
time: 109 us
  Pallas kernels  109 us (100%)
    pallas_call x1, Pallas kernels, body(): pl.pallas_call(kernel, out_shape=[vmem(*shape) for shape in shapes], in_s...  107 us
    pallas_call x1, Pallas kernels, body(): pl.pallas_call(last_update, out_shape=jax.ShapeDtypeStruct((rows, columns...  2.66 us

profile of v8, /device:TPU:1, one launch (start us, length us, event | category | flops | bytes accessed | tf_op | source)
XLA Modules:
  0.0 109.4 jit_solution(11971761602914930909)
XLA Ops:
  0.0 106.7 %shard_map.37 = (f32[2048,512]{1,0:T(8,128)S(1)}, bf16[2048,256]{1,0:T(8,128)(2,1)S(1)}, bf16[2048,256]{1,0:T(8,128)(2,1)S(1)}, bf16[256,512]{1,0:T(8,128)(2,1)S(1)}, bf16[256,512]{1,0:T(8,128)(2,1)S(1)}) custom-call(f32[2048,512]{1,0:T(8,128)} %field_in.1, f32[4,4,8,2048]{3,2,1,0:T(8,128)} %bitcast.3, f32[4,256,256]{2,1,0:T(8,128)} %factor_in.1), custom_call_target="tpu_custom_call" | custom-call | flops 12000000000 | bytes 6291456 | tf_op jit(solution)/shard_map/pallas_call | solution.py:279
  106.7 2.7 %shard_map.38 = f32[2048,512]{1,0:T(8,128)} custom-call(f32[2048,512]{1,0:T(8,128)S(1)} %get-tuple-element.10.field, bf16[2048,256]{1,0:T(8,128)(2,1)S(1)} %get-tuple-element.11.plain_high, bf16[2048,256]{1,0:T(8,128)(2,1)S(1)} %get-tuple-element.12.plain_low, bf16[256,512]{1,0:T(8,128)(2,1)S(1)} %get-tuple-element.13.coef_high, ...), custom_call_target="tpu_custom_call" | custom-call | flops 2000000000 | bytes 4194304 | tf_op jit(solution)/shard_map/pallas_call | solution.py:308
